TPU v7x, 32 devices: a whole 2x2x4 slice. The times are simulated.
32 devices in a mesh: dom: 16 (over z, y, core), grp: 2 (over x).
Axes of the slice: x: 2, y: 2, z: 4, core: 2. Of those that a mesh axis runs over, the one named last changes fastest.
Arguments:
- positions: float32 [3, 4096], P(None, ('dom', 'grp')), may hold values from 0 to 1
- features: bfloat16 [128, 4096], P(None, ('dom', 'grp')), may hold values from -6 to 6
- neighbour_weight: bfloat16 [128, 128], replicated, may hold values from -0.5 to 0.5
- adjoint: bfloat16 [256, 4096], P(None, ('dom', 'grp')), may hold values from -0.119628906 to 0.119628906
- basis_weight: bfloat16 [8, 128], replicated, may hold values from -2 to 2
- edge_weight: bfloat16 [128, 64], replicated, may hold values from -0.5 to 0.5
- tile_center: int32 [128], P(('dom', 'grp')), may hold values from 0 to 1
- tile_neighbour: int32 [128], P(('dom', 'grp')), may hold values from 0 to 5, as said below
- tile_count: int32 [32], P(('dom', 'grp')), may hold values from 2 to 4, as said below
Outputs:
- position_grad: float32 [3, 4096], P(None, ('dom', 'grp'))
Inputs may be any that keep to these rules, and one draw needn't show every extreme that they name: `tile_count`: some device has all 4 slots live in every draw. `tile_neighbour`: the first slot of every device with an even index s names a block of the lower domain, that of every odd device a block of the upper domain; other slots are uniform over the three domains.
All inputs are finite; a program needn't handle non-finite values.
Results may differ from a plain program's by a relative error of at most 0.0012.
Values may be sent and summed in bfloat16 or wider, within the bound.
No kernel may reach another device: no remote copies, remote signals or barrier semaphores. Data moves between devices by JAX's collectives and lax.ppermute only.
A program may use at most 64 MiB of HBM per device.

v0:
```python
import functools
import math

import jax
import jax.numpy as jnp
from jax import lax
from jax.experimental import pallas as pl
from jax.experimental.pallas import tpu as pltpu
from jax.sharding import PartitionSpec as P

slab_length = 1.0
cutoff_square = 4.0
F32 = jnp.float32
BF16 = jnp.bfloat16
COLUMN_STEP = 8
PAD_ROWS = 16


def turned(value, by):
    count = lax.axis_size("grp")
    return lax.ppermute(value, "grp", [((i + by) % count, i) for i in range(count)])


def swapped(value, side):
    count = lax.axis_size("dom")
    pairs = []
    for i in range(0, count, 2):
        other = (i + 1 - 2 * side) % count
        pairs += [(i, other), (other, i)]
    return lax.ppermute(value, "dom", pairs)


def pack_kernel(
    positions, features, adjoint, tile_center, tile_neighbour, tile_count, packed, whole, coords,
    lists, counts, sems,
):
    latent, block = features.shape
    slots = tile_center.shape[0]
    copies = [
        pltpu.make_async_copy(source, target, sems.at[n])
        for n, (source, target) in enumerate(
            [
                (features, packed.at[0:latent]),
                (features, whole.at[0:latent]),
                (adjoint, whole.at[latent + PAD_ROWS : whole.shape[0]]),
                (positions, coords),
                (tile_center, lists.at[0]),
                (tile_neighbour, lists.at[1]),
                (tile_count, counts),
            ]
        )
    ]
    for copy in copies:
        copy.start()
    for copy in copies[3:]:
        copy.wait()
    values = coords[...]
    high = values.astype(BF16).astype(F32)
    rest = values - high
    middle = rest.astype(BF16).astype(F32)
    low = rest - middle
    lane = lax.broadcasted_iota(jnp.int32, (1, block), 1)
    listed = jnp.where(lane == 2 * slots, counts[0], 0)
    for slot in range(slots):
        listed = jnp.where(lane == slot, lists[0, slot], listed)
        listed = jnp.where(lane == slots + slot, lists[1, slot], listed)
    parts = [high, middle, low, listed.astype(F32), jnp.zeros((PAD_ROWS - 10, block), F32)]
    parts = jnp.concatenate(parts, axis=0).astype(BF16)
    packed[latent : latent + PAD_ROWS, :] = parts
    whole[latent : latent + PAD_ROWS, :] = parts
    for copy in copies[:3]:
        copy.wait()


def tiles_kernel(groups, slots, far, listed_far, own, side, weights, earlier, results, scratch):
    (neighbour_weight, basis_weight, edge_weight) = weights
    (half_neigh, pos, half_own, dist, env_harm, displace, keep_inner, radial, along, listed,
     listed_smem, sem, tally, work, *extra) = scratch
    if far:
        mixed, cols, _, earlier_neigh = earlier
        *shares, far_out, near_out, own_sums = results
        neigh_sums = extra[0]
    else:
        mixed, cols, own_sums, neigh_sums, far_work = results
    latent, block = neighbour_weight.shape
    basis_count = basis_weight.shape[0]
    channels = edge_weight.shape[0]
    rows = block // groups
    packed_rows = latent + PAD_ROWS
    window = 3 * groups
    member = lax.axis_index("grp")
    near_slab = 2 - 2 * lax.rem(lax.axis_index("dom"), 2)
    far_slab = 2 - near_slab
    side_slab = far_slab if far else near_slab

    if not far:
        for turn in range(groups):
            row = own[turn][latent : latent + PAD_ROWS, :].astype(F32)[8:16, :]
            listed[turn * 8 : turn * 8 + 8, :] = row.astype(jnp.int32)
        to_scalars = pltpu.make_async_copy(listed, listed_smem, sem)
        to_scalars.start()

    third = lax.broadcasted_iota(jnp.int32, (8, block), 0) == 2
    zero5 = jnp.zeros((5, block), F32)

    def coords_of(part):
        return jnp.concatenate([part[0:3] + part[3:6] + part[6:9], zero5], axis=0)

    def neighbour(index, ref, start, lift):
        product = lax.dot_general(
            neighbour_weight[...],
            ref[start : start + latent, :],
            (((0,), (0,)), ((), ())),
            preferred_element_type=F32,
        )
        half_neigh[index] = product.astype(BF16) * 0.5
        part = ref[start + latent : start + packed_rows, :].astype(F32)
        pos[index] = coords_of(part) + jnp.where(third, lift, 0.0)

    lift = jnp.asarray(side_slab - 1, jnp.int32).astype(F32) * slab_length
    neighbour(groups, side, 0, lift)
    if not far:
        for turn in range(groups):
            neighbour(turn, own[turn], 0, 0.0)

    sub8 = lax.broadcasted_iota(jnp.int32, (8, block), 0)
    rates = jnp.zeros((8, block), F32)
    for b in range(basis_count):
        rates = jnp.where(sub8 == b, 0.3 * 1.5**b, rates)
    weight_rows = basis_weight[...].astype(F32) * 0.5
    rated_rows = weight_rows * rates
    exponents = rates * (-math.log2(math.e))
    lane = lax.broadcasted_iota(jnp.int32, (latent, block), 1)
    weight_cols = (
        jnp.concatenate([weight_rows, jnp.zeros((block - basis_count, latent), F32)], axis=0)
        .T
    )
    eye = jnp.where(
        lax.broadcasted_iota(jnp.int32, (latent, latent), 0)
        == lax.broadcasted_iota(jnp.int32, (latent, latent), 1),
        1.0,
        0.0,
    ).astype(BF16)
    for turn in range(groups):
        half_own[turn] = own[turn][0:latent, :].astype(F32) * 0.5
        if far:
            continue
        own_sums[3 * turn : 3 * turn + 3] = jnp.zeros((3, block, block), F32)
        for m in range(4):
            at = (turn * 8 + m) * block
            mixed[at : at + block, :] = lax.dot_general(
                own[turn][packed_rows + m * channels : packed_rows + (m + 1) * channels, :],
                edge_weight[...],
                (((0,), (0,)), ((), ())),
                preferred_element_type=F32,
            )
            at = (turn * 8 + 4 + m) * block
            mixed[at : at + block, :] = jnp.zeros((block, latent), F32)
        part = own[turn][latent : latent + PAD_ROWS, :].astype(F32)
        column = jnp.concatenate(
            [coords_of(part), jnp.zeros((block - 8, block), F32)], axis=0
        ).T
        for axis in range(3):
            cols[turn * 3 + axis] = jnp.broadcast_to(column[:, axis : axis + 1], (block, block))
    neigh_sums[...] = jnp.zeros_like(neigh_sums)

    if not far:
        for entry in range(groups * window):
            tally[entry] = 0
        to_scalars.wait()
        for turn in range(groups):
            at = turn * 8 + 1
            count = listed_smem[at, 2 * slots]
            for slot in range(slots):
                entry = listed_smem[at, slot] * window + listed_smem[at, slots + slot]
                tally[entry] += jnp.where(slot < count, 1, 0)

        def copies_of(center, slab, b):
            return tally[center * window + slab * groups + b]

        def live(center, slab, b):
            return jnp.where(copies_of(center, slab, b) > 0, 1, 0)

        pool = sum(live(center, 1, b) for center in range(groups) for b in range(groups))
        fixed = [
            sum(live(center, slab, b) for center in range(groups) for slab in (0, 2))
            for b in range(groups)
        ]
        target = pool + sum(fixed)
        begin, end, edge = jnp.int32(0), jnp.int32(0), jnp.int32(0)
        for b in range(groups):
            following = jnp.minimum(
                edge + jnp.maximum(target - groups * fixed[b], 0), groups * pool
            )
            begin = jnp.where(member == b, edge, begin)
            end = jnp.where(member == b, following, end)
            edge = following
        units = jnp.int32(0)
        for center in range(groups):
            turn = lax.rem(center - member + groups, groups)
            work[0, units] = turn
            work[2, units] = groups
            work[3, units] = copies_of(center, near_slab, member)
            units = units + live(center, near_slab, member)
        whole_units = units
        place = jnp.int32(0)
        for center in range(groups):
            turn = lax.rem(center - member + groups, groups)
            for b in range(groups):
                for part in range(groups):
                    work[0, units] = turn
                    work[1, units] = part
                    work[2, units] = lax.rem(b - member + groups, groups)
                    work[3, units] = copies_of(center, 1, b)
                    mine = jnp.logical_and(place >= begin, place < end)
                    units = units + jnp.where(mine, live(center, 1, b), 0)
                    place = place + live(center, 1, b)
        far_units = jnp.int32(0)
        for center in range(groups):
            far_work[1 + far_units * 2] = lax.rem(center - member + groups, groups)
            far_work[2 + far_units * 2] = copies_of(center, far_slab, member)
            far_units = far_units + live(center, far_slab, member)
        far_work[0] = far_units
    else:
        units = whole_units = listed_far[0]

    def run_unit(rows, unit, carry):
        if far:
            center_turn = listed_far[1 + unit * 2]
            first_row = 0
            copies = listed_far[2 + unit * 2].astype(F32)
            index = groups
            self_pair = jnp.float32(0.0)
        else:
            center_turn = work[0, unit]
            first_row = pl.multiple_of(work[1, unit] * rows, rows) if rows < block else 0
            index = work[2, unit]
            copies = work[3, unit].astype(F32)
            self_pair = jnp.where(center_turn == index, 1.0, 0.0).astype(F32)

        square = None
        steps = []
        for axis in range(3):
            step = (
                pos[index, axis : axis + 1, :]
                - cols[center_turn * 3 + axis, pl.ds(first_row, rows), :]
            )
            steps.append(step)
            square = step * step if square is None else square + step * step
        same = (
            lax.broadcasted_iota(jnp.int32, (rows, block), 0) + first_row
            == lax.broadcasted_iota(jnp.int32, (rows, block), 1)
        )
        keep = 1.0 - self_pair * jnp.where(same, 1.0, 0.0)
        inner = jnp.maximum(1.0 - square * (1.0 / cutoff_square), 0.0) * keep
        envelope = inner * inner
        dist[0:rows, :] = square
        keep_inner[0:rows, :] = inner
        env_harm[0:rows, :] = envelope
        for axis in range(3):
            displace[axis, 0:rows, :] = steps[axis]
            env_harm[(axis + 1) * rows : (axis + 2) * rows, :] = envelope * (steps[axis] * 0.5)
        half_n = half_neigh[index]
        rest = jnp.concatenate([jnp.zeros((block - 2 * basis_count, block), BF16), half_n], axis=0)
        rest = jnp.concatenate([rest, rest], axis=1)
        half_center = half_own[center_turn]

        for chunk in range(rows // COLUMN_STEP):
            first = chunk * COLUMN_STEP
            shift = lax.rem(2 * block - first_row - first + basis_count, block)
            rolled = pltpu.roll(half_center, shift, 1)
            rolled = jnp.where(lane < basis_count, weight_cols, rolled)
            rolled = jnp.where(lane < 2 * basis_count, rolled, 0.0)
            left = jnp.concatenate([rolled.astype(BF16), eye], axis=1)
            for k in range(0, COLUMN_STEP, 2):
                right = []
                basis = []
                for e in (k, k + 1):
                    vals = jnp.exp2(exponents * dist[first + e : first + e + 1, :])
                    basis.append(vals)
                    onehot = jnp.where(sub8 == e, 1.0, 0.0)
                    right.append(jnp.concatenate([vals, onehot], axis=0).astype(BF16))
                right = jnp.concatenate([jnp.concatenate(right, axis=1), rest], axis=0)
                pre = jnp.dot(left, right, preferred_element_type=F32)
                for n, e in enumerate((k, k + 1)):
                    half = pre[:, n * block : (n + 1) * block].astype(BF16)
                    tanh = jnp.tanh(half)
                    up = 1 + tanh
                    hidden = half * up
                    slope = up + hidden * (1 - tanh)
                    both = jnp.concatenate([slope, hidden], axis=0)
                    row = first + e
                    at = center_turn * (8 * block) + first_row + row
                    mix = [mixed[pl.ds(at + m * block, 1), :] for m in range(4)]
                    top = jnp.concatenate([mix[m] * rated_rows for m in range(4)], axis=0)
                    exact = mixed[pl.ds(at, 8, stride=block), :]
                    high = exact.astype(BF16).astype(F32)
                    low = jnp.concatenate([high, exact - high], axis=0)
                    lhs = jnp.concatenate(
                        [
                            jnp.concatenate([top, jnp.zeros((16, latent), F32)], axis=0),
                            jnp.concatenate([jnp.zeros((32, latent), F32), low], axis=0),
                        ],
                        axis=1,
                    ).astype(BF16)
                    out = jnp.dot(lhs, both, preferred_element_type=F32)
                    total = None
                    for m in range(4):
                        at = m * rows + row
                        term = env_harm[at : at + 1, :] * out[m * 8 : m * 8 + 8]
                        total = term if total is None else total + term
                    radial[row * 8 : row * 8 + 8, :] = total * basis[n]
                    along[row * 8 : row * 8 + 8, :] = out[32:40] + out[40:48]

        totals = [jnp.zeros((8, block), F32) for _ in range(3)]
        scale = copies * 2.0
        for part in range(rows // 8):
            at = slice(part * 8, part * 8 + 8)
            basis_part = None
            for b in range(basis_count):
                term = radial[pl.ds(part * 64 + b, 8, stride=8), :]
                basis_part = term if basis_part is None else basis_part + term
            alongs = [along[pl.ds(part * 64 + m, 8, stride=8), :] for m in range(4)]
            step = [displace[axis, at, :] for axis in range(3)]
            env_grad = alongs[0] + 0.5 * (
                alongs[1] * step[0] + alongs[2] * step[1] + alongs[3] * step[2]
            )
            square_grad = -basis_part - env_grad * keep_inner[at, :] * (2.0 / cutoff_square)
            half_env = (0.5 * copies) * env_harm[at, :]
            square_grad = scale * square_grad
            at_center = pl.ds(pl.multiple_of(first_row + part * 8, 8), 8)
            for axis in range(3):
                grad = square_grad * step[axis] + half_env * alongs[axis + 1]
                totals[axis] = totals[axis] + grad
                own_sums[center_turn * 3 + axis, at_center, :] += grad
        for axis in range(3):
            neigh_sums[3 * index + axis] += totals[axis]
        return carry

    lax.fori_loop(0, whole_units, functools.partial(run_unit, block), 0)
    if not far:
        lax.fori_loop(whole_units, units, functools.partial(run_unit, rows), 0)
    if not far:
        return

    def column_sums(ref, index):
        return jnp.concatenate(
            [jnp.sum(ref[3 * index + axis], axis=0, keepdims=True) for axis in range(3)], axis=0
        )

    far_out[...] = column_sums(neigh_sums, groups)
    near_out[...] = column_sums(earlier_neigh, groups)
    for turn in range(groups):
        wide = jnp.zeros((block, block), F32)
        for axis in range(3):
            rows_sum = jnp.sum(own_sums[3 * turn + axis], axis=1, keepdims=True)
            wide = jnp.where(lane == axis, rows_sum, wide)
        shares[turn][...] = column_sums(earlier_neigh, turn) - wide.T[0:3, :]


def tiles_call(groups, slots, far, listed_far, own, side, weights, earlier):
    latent, block = weights[0].shape
    rows = block // groups
    vmem = pl.BlockSpec(memory_space=pltpu.VMEM)
    smem = pl.BlockSpec(memory_space=pltpu.SMEM)
    operands = [*own, side, *weights, *earlier]
    specs = [vmem] * len(operands)
    sums_shape = (3 * groups, block, block)
    if far:
        results = [jax.ShapeDtypeStruct((3, block), F32)] * (groups + 2)
        results.append(pltpu.VMEM(sums_shape, F32))
        operands = [listed_far] + operands
        specs = [smem] + specs
    else:
        shapes = [(8 * groups * block, latent), sums_shape, sums_shape, (3 * (groups + 1), 8, block)]
        results = [pltpu.VMEM(shape, F32) for shape in shapes]
        results.append(pltpu.SMEM((1 + 2 * (groups + 1),), jnp.int32))
    result_specs = [vmem] * len(results)
    if not far:
        result_specs[-1] = smem

    def body(*refs):
        refs = list(refs)
        take = lambda count: [refs.pop(0) for _ in range(count)]
        listed_ref = take(1)[0] if far else None
        own_refs = take(groups)
        (side_ref,) = take(1)
        weight_refs = take(3)
        earlier_refs = take(len(earlier))
        result_refs = take(len(results))
        tiles_kernel(
            groups, slots, far, listed_ref, own_refs, side_ref, weight_refs, earlier_refs,
            result_refs, refs,
        )

    tiles = groups * slots // (3 if far else 2)
    return pl.pallas_call(
        body,
        out_shape=results,
        in_specs=specs,
        out_specs=result_specs,
        input_output_aliases={len(operands) - 2: groups + 2} if far else {},
        scratch_shapes=[
            pltpu.VMEM((groups + 1, latent, block), BF16),
            pltpu.VMEM((groups + 1, 8, block), F32),
            pltpu.VMEM((groups, latent, block), F32),
            pltpu.VMEM((block, block), F32),
            pltpu.VMEM((4 * block, block), F32),
            pltpu.VMEM((3, block, block), F32),
            pltpu.VMEM((block, block), F32),
            pltpu.VMEM((8 * block, block), F32),
            pltpu.VMEM((8 * block, block), F32),
            pltpu.VMEM((8 * groups, block), jnp.int32),
            pltpu.SMEM((8 * groups, block), jnp.int32),
            pltpu.SemaphoreType.DMA,
            pltpu.SMEM((3 * groups * groups,), jnp.int32),
            pltpu.SMEM((4, groups * groups * (groups + 1) + 1), jnp.int32),
        ]
        + ([pltpu.VMEM((3 * (groups + 1), 8, block), F32)] if far else []),
        compiler_params=pltpu.CompilerParams(vmem_limit_bytes=32 * 1024 * 1024),
        cost_estimate=pl.CostEstimate(
            flops=tiles * rows * block * latent * 200,
            bytes_accessed=sum(x.size * x.dtype.itemsize for x in operands),
            transcendentals=tiles * rows * block * latent,
        ),
        name="far_tiles" if far else "near_tiles",
    )(*operands)


def on_device(
    positions,
    features,
    neighbour_weight,
    adjoint,
    basis_weight,
    edge_weight,
    tile_center,
    tile_neighbour,
    tile_count,
):
    groups = lax.axis_size("grp")
    latent, block = features.shape
    slots = tile_center.shape[0]
    packed_rows = latent + PAD_ROWS
    packed, whole = pl.pallas_call(
        pack_kernel,
        out_shape=[
            pltpu.VMEM((packed_rows, block), BF16),
            pltpu.VMEM((packed_rows + adjoint.shape[0], block), BF16),
        ],
        in_specs=[pl.BlockSpec(memory_space=pl.ANY)] * 6,
        out_specs=[pl.BlockSpec(memory_space=pltpu.VMEM)] * 2,
        scratch_shapes=[
            pltpu.VMEM(positions.shape, F32),
            pltpu.SMEM((2, slots), jnp.int32),
            pltpu.SMEM((1,), jnp.int32),
            pltpu.SemaphoreType.DMA((7,)),
        ],
        name="pack_rows",
    )(positions, features, adjoint, tile_center, tile_neighbour, tile_count)
    own = [whole] + [turned(whole, turn) for turn in range(1, groups)]
    near = swapped(packed, 0)
    far = swapped(packed, 1)
    weights = (neighbour_weight, basis_weight, edge_weight.T)
    *kept, far_work = tiles_call(groups, slots, False, None, own, near, weights, [])
    *shares, far_sum, near_sum, _ = tiles_call(
        groups, slots, True, far_work, own, far, weights, kept
    )
    total = shares[0] + swapped(far_sum, 1) + swapped(near_sum, 0)
    for turn in range(1, groups):
        total = total + turned(shares[turn], -turn)
    return total


def solution(mesh):
    placed = (
        P(None, ("dom", "grp")),
        P(None, ("dom", "grp")),
        P(),
        P(None, ("dom", "grp")),
        P(),
        P(),
        P(("dom", "grp")),
        P(("dom", "grp")),
        P(("dom", "grp")),
    )
    return jax.shard_map(
        on_device, mesh=mesh, in_specs=placed, out_specs=P(None, ("dom", "grp")), check_vma=False
    )
```

profile of v0, /device:TPU:0, one launch (start us, length us, event | category | flops | bytes accessed | tf_op | source)
XLA Modules:
  0.0 27.1 jit_solution(8558111249072469264)
XLA Ops:
  0.7 0.0 copy-start
  0.7 0.0 copy-start.1
  0.7 0.9 %pack_rows.1 = (bf16[144,128]{1,0:T(8,128)(2,1)S(1)}, bf16[400,128]{1,0:T(8,128)(2,1)S(1)}) custom-call(f32[3,128]{1,0:T(4,128)} %positions.1, bf16[128,128]{1,0:T(8,128)(2,1)} %features.1, bf16[256,128]{1,0:T(8,128)(2,1)} %adjoint.1, s32[4]{0:T(128)} %tile_center.1, s32[4]{0:T(128)} %tile_neighbour.1, s32[1]{0:T(128)S(6)} %copy.12.tile_count), custom_call_target="tpu_custom_call" | custom-call | tf_op jit(solution)/shard_map/pack_rows/pallas_call | solution.py:445
  1.6 0.0 copy-start.2
  1.6 3.0 %collective-permute-start = (bf16[400,128]{1,0:T(8,128)(2,1)S(1)}, bf16[400,128]{1,0:T(8,128)(2,1)S(1)}, u32[]{:S(2)}, u32[]{:S(2)}) collective-permute-start(bf16[400,128]{1,0:T(8,128)(2,1)S(1)} %get-tuple-element.16.refs_0_.refs_1_), channel_id=1, source_target_pairs={{1,0},{0,1},{3,2},{2,3},{5,4},{4,5},{7,6},{6,7},{9,8},{8,9},{11,10... | collective-permute-start | bytes 307208 | tf_op jit(solution)/shard_map/ppermute | solution.py:21
  4.6 0.0 collective-permute-start.1
  4.6 4.7 %collective-permute-start.2 = (bf16[144,128]{1,0:T(8,128)(2,1)S(1)}, bf16[144,128]{1,0:T(8,128)(2,1)S(1)}, u32[]{:S(2)}, u32[]{:S(2)}) collective-permute-start(bf16[144,128]{1,0:T(8,128)(2,1)S(1)} %get-tuple-element.17), channel_id=1, source_target_pairs={{0,30},{30,0},{4,2},{2,4},{8,6},{6,8},{12,10},{10,12},{16,14},{14,... | collective-permute-start | bytes 110600 | tf_op jit(solution)/shard_map/ppermute | solution.py:30
  9.3 0.0 collective-permute-done.1.refs_2_
  9.3 0.0 collective-permute-done.refs_1_.refs_2_
  9.3 0.0 copy-done
  9.3 0.0 copy-done.1
  9.3 0.0 copy-done.2
  9.3 6.7 %near_tiles.1 = (f32[2048,128]{1,0:T(8,128)S(1)}, f32[6,128,128]{2,1,0:T(8,128)S(1)}, f32[6,128,128]{2,1,0:T(8,128)S(1)}, f32[9,8,128]{2,1,0:T(8,128)S(1)}, s32[7]{0:T(128)S(4)}) custom-call(bf16[400,128]{1,0:T(8,128)(2,1)S(1)} %get-tuple-element.16.refs_0_.refs_1_, bf16[400,128]{1,0:T(8,128)(2,1)S(1)} %collective-permute-done.refs_1_.refs_2_, ...), custom_call_target="tpu_custom_call" | custom-call | flops 838860800 | bytes 292864 | tf_op jit(solution)/shard_map/near_tiles/pallas_call | solution.py:397
  16.0 0.0 collective-permute-done.2.refs_3_
  16.0 3.2 %far_tiles.1 = (f32[3,128]{1,0:T(4,128)S(1)}, f32[3,128]{1,0:T(4,128)S(1)}, f32[3,128]{1,0:T(4,128)S(1)}, f32[3,128]{1,0:T(4,128)S(1)}, f32[6,128,128]{2,1,0:T(8,128)S(1)}) custom-call(s32[7]{0:T(128)S(4)} %get-tuple-element.18.refs_0_, bf16[400,128]{1,0:T(8,128)(2,1)S(1)} %get-tuple-element.16.refs_0_.refs_1_, ...), custom_call_target="tpu_custom_call", output_to_operand_aliasing={{4}: (9, {})} | custom-call | flops 419430400 | bytes 2164764 | tf_op jit(solution)/shard_map/far_tiles/pallas_call | solution.py:397
  19.3 3.0 %collective-permute-start.3 = (f32[3,128]{1,0:T(4,128)S(1)}, f32[3,128]{1,0:T(4,128)S(1)}, u32[]{:S(2)}, u32[]{:S(2)}) collective-permute-start(f32[3,128]{1,0:T(4,128)S(1)} %get-tuple-element.24), channel_id=1, source_target_pairs={{0,30},{30,0},{4,2},{2,4},{8,6},{6,8},{12,10},{10,12},{16,14},{14,... | collective-permute-start | bytes 4616 | tf_op jit(solution)/shard_map/ppermute | solution.py:30
  22.3 0.6 %collective-permute-start.4 = (f32[3,128]{1,0:T(4,128)S(1)}, f32[3,128]{1,0:T(4,128)S(1)}, u32[]{:S(2)}, u32[]{:S(2)}) collective-permute-start(f32[3,128]{1,0:T(4,128)S(1)} %get-tuple-element.25), channel_id=1, source_target_pairs={{0,2},{2,0},{4,6},{6,4},{8,10},{10,8},{12,14},{14,12},{16,18},{18,... | collective-permute-start | bytes 4616 | tf_op jit(solution)/shard_map/ppermute | solution.py:30
  22.9 1.2 %collective-permute-start.5 = (f32[3,128]{1,0:T(4,128)S(1)}, f32[3,128]{1,0:T(4,128)S(1)}, u32[]{:S(2)}, u32[]{:S(2)}) collective-permute-start(f32[3,128]{1,0:T(4,128)S(1)} %get-tuple-element.26), channel_id=1, source_target_pairs={{1,0},{0,1},{3,2},{2,3},{5,4},{4,5},{7,6},{6,7},{9,8},{8,9},{11,10... | collective-permute-start | bytes 4616 | tf_op jit(solution)/shard_map/ppermute | solution.py:21
  24.1 1.0 %collective-permute-done.3 = f32[3,128]{1,0:T(4,128)S(1)} collective-permute-done((f32[3,128]{1,0:T(4,128)S(1)}, f32[3,128]{1,0:T(4,128)S(1)}, u32[]{:S(2)}, u32[]{:S(2)}) %collective-permute-start.3) | collective-permute-done | bytes 1568 | tf_op jit(solution)/shard_map/ppermute | solution.py:30
  25.1 0.0 collective-permute-done.4
  25.1 1.4 %collective-permute-done.5 = f32[3,128]{1,0:T(4,128)S(1)} collective-permute-done((f32[3,128]{1,0:T(4,128)S(1)}, f32[3,128]{1,0:T(4,128)S(1)}, u32[]{:S(2)}, u32[]{:S(2)}) %collective-permute-start.5) | collective-permute-done | bytes 1568 | tf_op jit(solution)/shard_map/ppermute | solution.py:21
  26.5 0.6 %add_add_fusion = f32[3,128]{1,0:T(4,128)} fusion(f32[3,128]{1,0:T(4,128)S(1)} %collective-permute-done.5, f32[3,128]{1,0:T(4,128)S(1)} %collective-permute-done.4, f32[3,128]{1,0:T(4,128)S(1)} %get-tuple-element.23, f32[3,128]{1,0:T(4,128)S(1)} %collective-permute-done.3), kind=kLoop, calls=%fused_computation | loop fusion | flops 1152 | bytes 7680 | tf_op jit(solution)/shard_map/add | solution.py:471
Async XLA Ops:
  0.7 8.7 %copy-start = (bf16[128,128]{1,0:T(8,128)(2,1)S(1)}, bf16[128,128]{1,0:T(8,128)(2,1)}, u32[]{:S(2)}) copy-start(bf16[128,128]{1,0:T(8,128)(2,1)} %refs_4_.3) | copy-start | bytes 98308
  0.7 8.7 %copy-start.1 = (bf16[128,64]{0,1:T(8,128)(2,1)S(1)}, bf16[128,64]{0,1:T(8,128)(2,1)}, u32[]{:S(2)}) copy-start(bf16[128,64]{0,1:T(8,128)(2,1)} %param.14) | copy-start | bytes 49156
  1.6 7.7 %copy-start.2 = (bf16[8,128]{1,0:T(8,128)(2,1)S(1)}, bf16[8,128]{1,0:T(8,128)(2,1)}, u32[]{:S(2)}) copy-start(bf16[8,128]{1,0:T(8,128)(2,1)} %refs_5_.1) | copy-start | bytes 6148
  1.6 7.7 %collective-permute-start = (bf16[400,128]{1,0:T(8,128)(2,1)S(1)}, bf16[400,128]{1,0:T(8,128)(2,1)S(1)}, u32[]{:S(2)}, u32[]{:S(2)}) collective-permute-start(bf16[400,128]{1,0:T(8,128)(2,1)S(1)} %get-tuple-element.16.refs_0_.refs_1_), channel_id=1, source_target_pairs={{1,0},{0,1},{3,2},{2,3},{5,4},{4,5},{7,6},{6,7},{9,8},{8,9},{11,10... | collective-permute-start | bytes 307208 | tf_op jit(solution)/shard_map/ppermute | solution.py:21
  4.6 4.7 %collective-permute-start.1 = (bf16[144,128]{1,0:T(8,128)(2,1)S(1)}, bf16[144,128]{1,0:T(8,128)(2,1)S(1)}, u32[]{:S(2)}, u32[]{:S(2)}) collective-permute-start(bf16[144,128]{1,0:T(8,128)(2,1)S(1)} %get-tuple-element.17), channel_id=1, source_target_pairs={{0,2},{2,0},{4,6},{6,4},{8,10},{10,8},{12,14},{14,12},{16,18},{18,... | collective-permute-start | bytes 110600 | tf_op jit(solution)/shard_map/ppermute | solution.py:30
  4.6 11.4 %collective-permute-start.2 = (bf16[144,128]{1,0:T(8,128)(2,1)S(1)}, bf16[144,128]{1,0:T(8,128)(2,1)S(1)}, u32[]{:S(2)}, u32[]{:S(2)}) collective-permute-start(bf16[144,128]{1,0:T(8,128)(2,1)S(1)} %get-tuple-element.17), channel_id=1, source_target_pairs={{0,30},{30,0},{4,2},{2,4},{8,6},{6,8},{12,10},{10,12},{16,14},{14,... | collective-permute-start | bytes 110600 | tf_op jit(solution)/shard_map/ppermute | solution.py:30
  19.3 5.8 %collective-permute-start.3 = (f32[3,128]{1,0:T(4,128)S(1)}, f32[3,128]{1,0:T(4,128)S(1)}, u32[]{:S(2)}, u32[]{:S(2)}) collective-permute-start(f32[3,128]{1,0:T(4,128)S(1)} %get-tuple-element.24), channel_id=1, source_target_pairs={{0,30},{30,0},{4,2},{2,4},{8,6},{6,8},{12,10},{10,12},{16,14},{14,... | collective-permute-start | bytes 4616 | tf_op jit(solution)/shard_map/ppermute | solution.py:30
  22.3 2.8 %collective-permute-start.4 = (f32[3,128]{1,0:T(4,128)S(1)}, f32[3,128]{1,0:T(4,128)S(1)}, u32[]{:S(2)}, u32[]{:S(2)}) collective-permute-start(f32[3,128]{1,0:T(4,128)S(1)} %get-tuple-element.25), channel_id=1, source_target_pairs={{0,2},{2,0},{4,6},{6,4},{8,10},{10,8},{12,14},{14,12},{16,18},{18,... | collective-permute-start | bytes 4616 | tf_op jit(solution)/shard_map/ppermute | solution.py:30
  22.9 3.6 %collective-permute-start.5 = (f32[3,128]{1,0:T(4,128)S(1)}, f32[3,128]{1,0:T(4,128)S(1)}, u32[]{:S(2)}, u32[]{:S(2)}) collective-permute-start(f32[3,128]{1,0:T(4,128)S(1)} %get-tuple-element.26), channel_id=1, source_target_pairs={{1,0},{0,1},{3,2},{2,3},{5,4},{4,5},{7,6},{6,7},{9,8},{8,9},{11,10... | collective-permute-start | bytes 4616 | tf_op jit(solution)/shard_map/ppermute | solution.py:21
where the time goes:
time: 26.7 us; the launch traced here: 27.1 us
  starting transfers between devices  12.4 us (46%)
  Pallas kernels  10.9 us (41%)
  waiting for transfers between devices  2.43 us (9%)
  between operations  0.73 us (3%)
  other arithmetic  0.58 us (2%)
    pallas_call x2, Pallas kernels, tiles_call(): pl.pallas_call(body, out_shape=results, in_specs=specs, out_specs=result_...  9.92 us
    ppermute x4, starting transfers between devices, swapped(): return lax.ppermute(value, 'dom', pairs)  8.26 us
    ppermute x2, starting transfers between devices, turned(): lax.ppermute(value, 'grp', [((i + by) % count, i) for i in range(count)])  4.16 us
    ppermute x2, waiting for transfers between devices, turned(): lax.ppermute(value, 'grp', [((i + by) % count, i) for i in range(count)])  1.4 us
    ppermute x4, waiting for transfers between devices, swapped(): return lax.ppermute(value, 'dom', pairs)  1.03 us
    pallas_call x1, Pallas kernels, on_device(): pl.pallas_call(pack_kernel, out_shape=[pltpu.VMEM((packed_rows, block), B...  0.95 us
    add x1, other arithmetic, on_device(): total = total + turned(shares[turn], -turn)  0.58 us
  transfers between devices with their start and end apart: 6, of which 2 were waited for; matrix products, arithmetic and copies ran while one was open for 0% of the time, Pallas kernels for 25%

commit v1 on v0

--- a/solution.py
+++ b/solution.py
@@ -72,16 +72,20 @@
         copy.wait()
 
 
-def tiles_kernel(groups, slots, far, listed_far, own, side, weights, earlier, results, scratch):
+def tiles_kernel(groups, slots, stage, listed_far, own, side, weights, earlier, results, scratch):
     (neighbour_weight, basis_weight, edge_weight) = weights
-    (half_neigh, pos, half_own, dist, env_harm, displace, keep_inner, radial, along, listed,
-     listed_smem, sem, tally, work, *extra) = scratch
+    far = stage == "far"
     if far:
-        mixed, cols, _, earlier_neigh = earlier
+        mixed, cols, _, earlier_neigh, half_own = earlier
         *shares, far_out, near_out, own_sums = results
-        neigh_sums = extra[0]
+        (half_neigh, pos, neigh_sums, dist, env_harm, displace, keep_inner, radial, along) = scratch
     else:
-        mixed, cols, own_sums, neigh_sums, far_work = results
+        mixed, cols, own_sums, neigh_sums, half_own, half_neigh, pos, *far_work = results
+        if stage == "near":
+            (far_work,) = far_work
+            (dist, env_harm, displace, keep_inner, radial, along, listed, listed_smem, sem, tally,
+             work) = scratch
+    prepared = {"ahead": range(1), "near": range(1, groups), "far": range(0)}[stage]
     latent, block = neighbour_weight.shape
     basis_count = basis_weight.shape[0]
     channels = edge_weight.shape[0]
@@ -93,7 +97,7 @@
     far_slab = 2 - near_slab
     side_slab = far_slab if far else near_slab
 
-    if not far:
+    if stage == "near":
         for turn in range(groups):
             row = own[turn][latent : latent + PAD_ROWS, :].astype(F32)[8:16, :]
             listed[turn * 8 : turn * 8 + 8, :] = row.astype(jnp.int32)
@@ -118,10 +122,10 @@
         pos[index] = coords_of(part) + jnp.where(third, lift, 0.0)
 
     lift = jnp.asarray(side_slab - 1, jnp.int32).astype(F32) * slab_length
-    neighbour(groups, side, 0, lift)
-    if not far:
-        for turn in range(groups):
-            neighbour(turn, own[turn], 0, 0.0)
+    if stage != "near":
+        neighbour(groups, side, 0, lift)
+    for turn in prepared:
+        neighbour(turn, own[turn], 0, 0.0)
 
     sub8 = lax.broadcasted_iota(jnp.int32, (8, block), 0)
     rates = jnp.zeros((8, block), F32)
@@ -141,10 +145,8 @@
         1.0,
         0.0,
     ).astype(BF16)
-    for turn in range(groups):
+    for turn in prepared:
         half_own[turn] = own[turn][0:latent, :].astype(F32) * 0.5
-        if far:
-            continue
         own_sums[3 * turn : 3 * turn + 3] = jnp.zeros((3, block, block), F32)
         for m in range(4):
             at = (turn * 8 + m) * block
@@ -162,7 +164,10 @@
         ).T
         for axis in range(3):
             cols[turn * 3 + axis] = jnp.broadcast_to(column[:, axis : axis + 1], (block, block))
-    neigh_sums[...] = jnp.zeros_like(neigh_sums)
+    if stage != "near":
+        neigh_sums[...] = jnp.zeros_like(neigh_sums)
+    if stage == "ahead":
+        return
 
     if not far:
         for entry in range(groups * window):
@@ -276,7 +281,7 @@
                 right = []
                 basis = []
                 for e in (k, k + 1):
-                    vals = jnp.exp2(exponents * dist[first + e : first + e + 1, :])
+                    vals = jnp.exp2(exponents * dist[pl.ds(first + e, 8, stride=0), :])
                     basis.append(vals)
                     onehot = jnp.where(sub8 == e, 1.0, 0.0)
                     right.append(jnp.concatenate([vals, onehot], axis=0).astype(BF16))
@@ -291,7 +296,7 @@
                     both = jnp.concatenate([slope, hidden], axis=0)
                     row = first + e
                     at = center_turn * (8 * block) + first_row + row
-                    mix = [mixed[pl.ds(at + m * block, 1), :] for m in range(4)]
+                    mix = [mixed[pl.ds(at + m * block, 8, stride=0), :] for m in range(4)]
                     top = jnp.concatenate([mix[m] * rated_rows for m in range(4)], axis=0)
                     exact = mixed[pl.ds(at, 8, stride=block), :]
                     high = exact.astype(BF16).astype(F32)
@@ -307,7 +312,7 @@
                     total = None
                     for m in range(4):
                         at = m * rows + row
-                        term = env_harm[at : at + 1, :] * out[m * 8 : m * 8 + 8]
+                        term = env_harm[pl.ds(at, 8, stride=0), :] * out[m * 8 : m * 8 + 8]
                         total = term if total is None else total + term
                     radial[row * 8 : row * 8 + 8, :] = total * basis[n]
                     along[row * 8 : row * 8 + 8, :] = out[32:40] + out[40:48]
@@ -358,72 +363,85 @@
         shares[turn][...] = column_sums(earlier_neigh, turn) - wide.T[0:3, :]
 
 
-def tiles_call(groups, slots, far, listed_far, own, side, weights, earlier):
+def tiles_call(groups, slots, stage, listed_far, own, side, weights, earlier):
+    far = stage == "far"
     latent, block = weights[0].shape
-    rows = block // groups
     vmem = pl.BlockSpec(memory_space=pltpu.VMEM)
     smem = pl.BlockSpec(memory_space=pltpu.SMEM)
-    operands = [*own, side, *weights, *earlier]
+    heads = ([listed_far] if far else []) + list(own) + ([] if side is None else [side])
+    operands = [*heads, *weights, *earlier]
     specs = [vmem] * len(operands)
     sums_shape = (3 * groups, block, block)
+    neigh_shape = (3 * (groups + 1), 8, block)
+    half_neigh = pltpu.VMEM((groups + 1, latent, block), BF16)
+    pos = pltpu.VMEM((groups + 1, 8, block), F32)
     if far:
         results = [jax.ShapeDtypeStruct((3, block), F32)] * (groups + 2)
         results.append(pltpu.VMEM(sums_shape, F32))
-        operands = [listed_far] + operands
-        specs = [smem] + specs
+        specs[0] = smem
     else:
-        shapes = [(8 * groups * block, latent), sums_shape, sums_shape, (3 * (groups + 1), 8, block)]
-        results = [pltpu.VMEM(shape, F32) for shape in shapes]
-        results.append(pltpu.SMEM((1 + 2 * (groups + 1),), jnp.int32))
+        shapes = [(8 * groups * block, latent), sums_shape, sums_shape, neigh_shape]
+        shapes.append((groups, latent, block))
+        results = [pltpu.VMEM(shape, F32) for shape in shapes] + [half_neigh, pos]
     result_specs = [vmem] * len(results)
-    if not far:
-        result_specs[-1] = smem
+    first = len(heads) + len(weights)
+    aliases = {}
+    if far:
+        aliases = {first + 2: groups + 2}
+    elif stage == "near":
+        aliases = {first + n: n for n in range(len(results))}
+        results = results + [pltpu.SMEM((1 + 2 * (groups + 1),), jnp.int32)]
+        result_specs = result_specs + [smem]
 
     def body(*refs):
         refs = list(refs)
         take = lambda count: [refs.pop(0) for _ in range(count)]
         listed_ref = take(1)[0] if far else None
-        own_refs = take(groups)
-        (side_ref,) = take(1)
+        own_refs = take(len(own))
+        side_ref = None if side is None else take(1)[0]
         weight_refs = take(3)
         earlier_refs = take(len(earlier))
         result_refs = take(len(results))
         tiles_kernel(
-            groups, slots, far, listed_ref, own_refs, side_ref, weight_refs, earlier_refs,
+            groups, slots, stage, listed_ref, own_refs, side_ref, weight_refs, earlier_refs,
             result_refs, refs,
         )
 
-    tiles = groups * slots // (3 if far else 2)
-    return pl.pallas_call(
-        body,
-        out_shape=results,
-        in_specs=specs,
-        out_specs=result_specs,
-        input_output_aliases={len(operands) - 2: groups + 2} if far else {},
-        scratch_shapes=[
-            pltpu.VMEM((groups + 1, latent, block), BF16),
-            pltpu.VMEM((groups + 1, 8, block), F32),
-            pltpu.VMEM((groups, latent, block), F32),
-            pltpu.VMEM((block, block), F32),
-            pltpu.VMEM((4 * block, block), F32),
+    scratch = []
+    if far:
+        scratch += [half_neigh, pos, pltpu.VMEM(neigh_shape, F32)]
+    if stage != "ahead":
+        scratch += [
+            pltpu.VMEM((block + 8, block), F32),
+            pltpu.VMEM((4 * block + 8, block), F32),
             pltpu.VMEM((3, block, block), F32),
             pltpu.VMEM((block, block), F32),
             pltpu.VMEM((8 * block, block), F32),
             pltpu.VMEM((8 * block, block), F32),
+        ]
+    if stage == "near":
+        scratch += [
             pltpu.VMEM((8 * groups, block), jnp.int32),
             pltpu.SMEM((8 * groups, block), jnp.int32),
             pltpu.SemaphoreType.DMA,
             pltpu.SMEM((3 * groups * groups,), jnp.int32),
             pltpu.SMEM((4, groups * groups * (groups + 1) + 1), jnp.int32),
         ]
-        + ([pltpu.VMEM((3 * (groups + 1), 8, block), F32)] if far else []),
+    tiles = {"ahead": 0, "near": groups * slots // 2, "far": groups * slots // 3}[stage]
+    return pl.pallas_call(
+        body,
+        out_shape=results,
+        in_specs=specs,
+        out_specs=result_specs,
+        input_output_aliases=aliases,
+        scratch_shapes=scratch,
         compiler_params=pltpu.CompilerParams(vmem_limit_bytes=32 * 1024 * 1024),
         cost_estimate=pl.CostEstimate(
-            flops=tiles * rows * block * latent * 200,
+            flops=(tiles * (block // groups) * 200 + 24 * latent) * block * latent,
             bytes_accessed=sum(x.size * x.dtype.itemsize for x in operands),
-            transcendentals=tiles * rows * block * latent,
+            transcendentals=tiles * (block // groups) * block * latent,
         ),
-        name="far_tiles" if far else "near_tiles",
+        name=stage + "_tiles",
     )(*operands)
 
 
@@ -462,9 +480,10 @@
     near = swapped(packed, 0)
     far = swapped(packed, 1)
     weights = (neighbour_weight, basis_weight, edge_weight.T)
-    *kept, far_work = tiles_call(groups, slots, False, None, own, near, weights, [])
+    ahead = tiles_call(groups, slots, "ahead", None, own[:1], near, weights, [])
+    *kept, far_work = tiles_call(groups, slots, "near", None, own, None, weights, ahead)
     *shares, far_sum, near_sum, _ = tiles_call(
-        groups, slots, True, far_work, own, far, weights, kept
+        groups, slots, "far", far_work, [], far, weights, kept[:5]
     )
     total = shares[0] + swapped(far_sum, 1) + swapped(near_sum, 0)
     for turn in range(1, groups):

time: 26.7 us -> 25.3 us (0.948)
  starting transfers between devices: 12.4 us -> 10.2 us
  waiting for transfers between devices: 2.43 us -> 3.24 us
    ppermute x4, starting transfers between devices: 8.26 us -> 4.78 us  [swapped(): return lax.ppermute(value, 'dom', pairs)]
    ppermute x4, waiting for transfers between devices: 1.03 us -> 3.23 us  [swapped(): return lax.ppermute(value, 'dom', pairs)]
    ppermute x2, waiting for transfers between devices: 1.4 us -> 0.01 us  [turned(): lax.ppermute(value, 'grp', [((i + by) % count, i) for i in range(count)])]
    ppermute x2, starting transfers between devices: 4.16 us -> 5.39 us  [turned(): lax.ppermute(value, 'grp', [((i + by) % count, i) for i in range(count)])]
    pallas_call x2 -> x3, Pallas kernels: 9.92 us -> 9.99 us  [tiles_call(): pl.pallas_call(body, out_shape=results, in_specs=specs, out_specs=result_...]
  transfers between devices with their start and end apart: 6 -> 6, of which waited for: 2 -> 1; matrix products, arithmetic and copies ran while one was open for 0% -> 0% of each run, Pallas kernels for 25% -> 26%
where the time goes in v1:
time: 25.3 us; the launch traced here: 25.7 us
  Pallas kernels  10.9 us (43%)
  starting transfers between devices  10.2 us (40%)
  waiting for transfers between devices  3.24 us (13%)
  between operations  0.74 us (3%)
  other arithmetic  0.58 us (2%)
    pallas_call x3, Pallas kernels, tiles_call(): pl.pallas_call(body, out_shape=results, in_specs=specs, out_specs=result_...  9.99 us
    ppermute x2, starting transfers between devices, turned(): lax.ppermute(value, 'grp', [((i + by) % count, i) for i in range(count)])  5.39 us
    ppermute x4, starting transfers between devices, swapped(): return lax.ppermute(value, 'dom', pairs)  4.78 us
    ppermute x4, waiting for transfers between devices, swapped(): return lax.ppermute(value, 'dom', pairs)  3.23 us
    pallas_call x1, Pallas kernels, on_device(): pl.pallas_call(pack_kernel, out_shape=[pltpu.VMEM((packed_rows, block), B...  0.95 us
    add x1, other arithmetic, on_device(): total = total + turned(shares[turn], -turn)  0.58 us
  transfers between devices with their start and end apart: 6, of which 1 were waited for; matrix products, arithmetic and copies ran while one was open for 0% of the time, Pallas kernels for 26%

profile of v1, /device:TPU:0, one launch (start us, length us, event | category | flops | bytes accessed | tf_op | source)
XLA Modules:
  0.0 25.7 jit_solution(7999299564740191111)
XLA Ops:
  0.7 0.0 copy-start
  0.7 0.0 copy-start.1
  0.7 0.9 %pack_rows.1 = (bf16[144,128]{1,0:T(8,128)(2,1)S(1)}, bf16[400,128]{1,0:T(8,128)(2,1)S(1)}) custom-call(f32[3,128]{1,0:T(4,128)} %positions.1, bf16[128,128]{1,0:T(8,128)(2,1)} %features.1, bf16[256,128]{1,0:T(8,128)(2,1)} %adjoint.1, s32[4]{0:T(128)} %tile_center.1, s32[4]{0:T(128)} %tile_neighbour.1, s32[1]{0:T(128)S(6)} %copy.26.tile_count), custom_call_target="tpu_custom_call" | custom-call | tf_op jit(solution)/shard_map/pack_rows/pallas_call | solution.py:463
  1.6 0.0 copy-start.2
  1.6 3.0 %collective-permute-start = (bf16[400,128]{1,0:T(8,128)(2,1)S(1)}, bf16[400,128]{1,0:T(8,128)(2,1)S(1)}, u32[]{:S(2)}, u32[]{:S(2)}) collective-permute-start(bf16[400,128]{1,0:T(8,128)(2,1)S(1)} %get-tuple-element.24.refs_0_), channel_id=1, source_target_pairs={{1,0},{0,1},{3,2},{2,3},{5,4},{4,5},{7,6},{6,7},{9,8},{8,9},{11,10... | collective-permute-start | bytes 307208 | tf_op jit(solution)/shard_map/ppermute | solution.py:21
  4.6 0.0 collective-permute-start.1
  4.6 4.7 %collective-permute-start.2 = (bf16[144,128]{1,0:T(8,128)(2,1)S(1)}, bf16[144,128]{1,0:T(8,128)(2,1)S(1)}, u32[]{:S(2)}, u32[]{:S(2)}) collective-permute-start(bf16[144,128]{1,0:T(8,128)(2,1)S(1)} %get-tuple-element.25), channel_id=1, source_target_pairs={{0,30},{30,0},{4,2},{2,4},{8,6},{6,8},{12,10},{10,12},{16,14},{14,... | collective-permute-start | bytes 110600 | tf_op jit(solution)/shard_map/ppermute | solution.py:30
  9.3 0.0 collective-permute-done.1.refs_1_
  9.3 0.0 copy-done
  9.3 0.0 copy-done.1
  9.3 0.0 copy-done.2
  9.3 0.3 %ahead_tiles.1 = (f32[2048,128]{1,0:T(8,128)S(1)}, f32[6,128,128]{2,1,0:T(8,128)S(1)}, f32[6,128,128]{2,1,0:T(8,128)S(1)}, f32[9,8,128]{2,1,0:T(8,128)S(1)}, f32...) custom-call(bf16[400,128]{1,0:T(8,128)(2,1)S(1)} %get-tuple-element.24.refs_0_, ...), custom_call_target="tpu_custom_call" | custom-call | flops 50331648 | bytes 190464 | tf_op jit(solution)/shard_map/ahead_tiles/pallas_call | solution.py:431
  9.7 0.0 collective-permute-done.refs_1_
  9.7 6.5 %near_tiles.1 = (f32[2048,128]{1,0:T(8,128)S(1)}, f32[6,128,128]{2,1,0:T(8,128)S(1)}, f32[6,128,128]{2,1,0:T(8,128)S(1)}, f32[9,8,128]{2,1,0:T(8,128)S(1)}, f32[...) custom-call(bf16[400,128]{1,0:T(8,128)(2,1)S(1)} %get-tuple-element., ...), custom_call_target="tpu_custom_call", output_to_operand_aliasing={{0}: (5, {}), {1}: (6, {}), {2}: (7, {}), {3}: (8, {}), {4}... | custom-call | flops 889192448 | bytes 2369536 | tf_op jit(solution)/shard_map/near_tiles/pallas_call | solution.py:431
  16.1 0.0 collective-permute-done.2.refs_1_
  16.2 3.2 %far_tiles.1 = (f32[3,128]{1,0:T(4,128)S(1)}, f32[3,128]{1,0:T(4,128)S(1)}, f32[3,128]{1,0:T(4,128)S(1)}, f32[3,128]{1,0:T(4,128)S(1)}, f32[6,128,128]{2,1,0:T(8,128)S(1)}) custom-call(s32[7]{0:T(128)S(4)} %get-tuple-element.33.refs_0_, bf16[144,128]{1,0:T(8,128)(2,1)S(1)} %collective-permute-done.2.refs_1_, ...), custom_call_target="tpu_custom_call", output_to_operand_aliasing={{4}: (7, {})} | custom-call | flops 469762048 | bytes 2091036 | tf_op jit(solution)/shard_map/far_tiles/pallas_call | solution.py:431
  19.4 0.0 collective-permute-start.3
  19.4 0.1 collective-permute-start.4
  19.5 2.4 %collective-permute-start.5 = (f32[3,128]{1,0:T(4,128)S(1)}, f32[3,128]{1,0:T(4,128)S(1)}, u32[]{:S(2)}, u32[]{:S(2)}) collective-permute-start(f32[3,128]{1,0:T(4,128)S(1)} %get-tuple-element.42), channel_id=1, source_target_pairs={{1,0},{0,1},{3,2},{2,3},{5,4},{4,5},{7,6},{6,7},{9,8},{8,9},{11,10... | collective-permute-start | bytes 4616 | tf_op jit(solution)/shard_map/ppermute | solution.py:21
  21.9 3.2 %collective-permute-done.3 = f32[3,128]{1,0:T(4,128)S(1)} collective-permute-done((f32[3,128]{1,0:T(4,128)S(1)}, f32[3,128]{1,0:T(4,128)S(1)}, u32[]{:S(2)}, u32[]{:S(2)}) %collective-permute-start.3) | collective-permute-done | bytes 1568 | tf_op jit(solution)/shard_map/ppermute | solution.py:30
  25.1 0.0 collective-permute-done.4
  25.1 0.0 collective-permute-done.5
  25.1 0.6 %add_add_fusion = f32[3,128]{1,0:T(4,128)} fusion(f32[3,128]{1,0:T(4,128)S(1)} %collective-permute-done.5, f32[3,128]{1,0:T(4,128)S(1)} %collective-permute-done.4, f32[3,128]{1,0:T(4,128)S(1)} %get-tuple-element.39, f32[3,128]{1,0:T(4,128)S(1)} %collective-permute-done.3), kind=kLoop, calls=%fused_computation | loop fusion | flops 1152 | bytes 7680 | tf_op jit(solution)/shard_map/add | solution.py:490
Async XLA Ops:
  0.7 8.7 %copy-start = (bf16[128,128]{1,0:T(8,128)(2,1)S(1)}, bf16[128,128]{1,0:T(8,128)(2,1)}, u32[]{:S(2)}) copy-start(bf16[128,128]{1,0:T(8,128)(2,1)} %refs_2_.5) | copy-start | bytes 98308
  0.7 8.7 %copy-start.1 = (bf16[128,64]{0,1:T(8,128)(2,1)S(1)}, bf16[128,64]{0,1:T(8,128)(2,1)}, u32[]{:S(2)}) copy-start(bf16[128,64]{0,1:T(8,128)(2,1)} %param.14) | copy-start | bytes 49156
  1.6 7.7 %copy-start.2 = (bf16[8,128]{1,0:T(8,128)(2,1)S(1)}, bf16[8,128]{1,0:T(8,128)(2,1)}, u32[]{:S(2)}) copy-start(bf16[8,128]{1,0:T(8,128)(2,1)} %refs_3_.5) | copy-start | bytes 6148
  1.6 8.0 %collective-permute-start = (bf16[400,128]{1,0:T(8,128)(2,1)S(1)}, bf16[400,128]{1,0:T(8,128)(2,1)S(1)}, u32[]{:S(2)}, u32[]{:S(2)}) collective-permute-start(bf16[400,128]{1,0:T(8,128)(2,1)S(1)} %get-tuple-element.24.refs_0_), channel_id=1, source_target_pairs={{1,0},{0,1},{3,2},{2,3},{5,4},{4,5},{7,6},{6,7},{9,8},{8,9},{11,10... | collective-permute-start | bytes 307208 | tf_op jit(solution)/shard_map/ppermute | solution.py:21
  4.6 4.7 %collective-permute-start.1 = (bf16[144,128]{1,0:T(8,128)(2,1)S(1)}, bf16[144,128]{1,0:T(8,128)(2,1)S(1)}, u32[]{:S(2)}, u32[]{:S(2)}) collective-permute-start(bf16[144,128]{1,0:T(8,128)(2,1)S(1)} %get-tuple-element.25), channel_id=1, source_target_pairs={{0,2},{2,0},{4,6},{6,4},{8,10},{10,8},{12,14},{14,12},{16,18},{18,... | collective-permute-start | bytes 110600 | tf_op jit(solution)/shard_map/ppermute | solution.py:30
  4.6 11.5 %collective-permute-start.2 = (bf16[144,128]{1,0:T(8,128)(2,1)S(1)}, bf16[144,128]{1,0:T(8,128)(2,1)S(1)}, u32[]{:S(2)}, u32[]{:S(2)}) collective-permute-start(bf16[144,128]{1,0:T(8,128)(2,1)S(1)} %get-tuple-element.25), channel_id=1, source_target_pairs={{0,30},{30,0},{4,2},{2,4},{8,6},{6,8},{12,10},{10,12},{16,14},{14,... | collective-permute-start | bytes 110600 | tf_op jit(solution)/shard_map/ppermute | solution.py:30
  19.4 5.7 %collective-permute-start.3 = (f32[3,128]{1,0:T(4,128)S(1)}, f32[3,128]{1,0:T(4,128)S(1)}, u32[]{:S(2)}, u32[]{:S(2)}) collective-permute-start(f32[3,128]{1,0:T(4,128)S(1)} %get-tuple-element.40), channel_id=1, source_target_pairs={{0,30},{30,0},{4,2},{2,4},{8,6},{6,8},{12,10},{10,12},{16,14},{14,... | collective-permute-start | bytes 4616 | tf_op jit(solution)/shard_map/ppermute | solution.py:30
  19.4 5.7 %collective-permute-start.4 = (f32[3,128]{1,0:T(4,128)S(1)}, f32[3,128]{1,0:T(4,128)S(1)}, u32[]{:S(2)}, u32[]{:S(2)}) collective-permute-start(f32[3,128]{1,0:T(4,128)S(1)} %get-tuple-element.41), channel_id=1, source_target_pairs={{0,2},{2,0},{4,6},{6,4},{8,10},{10,8},{12,14},{14,12},{16,18},{18,... | collective-permute-start | bytes 4616 | tf_op jit(solution)/shard_map/ppermute | solution.py:30
  19.5 5.6 %collective-permute-start.5 = (f32[3,128]{1,0:T(4,128)S(1)}, f32[3,128]{1,0:T(4,128)S(1)}, u32[]{:S(2)}, u32[]{:S(2)}) collective-permute-start(f32[3,128]{1,0:T(4,128)S(1)} %get-tuple-element.42), channel_id=1, source_target_pairs={{1,0},{0,1},{3,2},{2,3},{5,4},{4,5},{7,6},{6,7},{9,8},{8,9},{11,10... | collective-permute-start | bytes 4616 | tf_op jit(solution)/shard_map/ppermute | solution.py:21
